TPU v7x, 256 devices: a whole 4x4x8 slice. The times are simulated.
256 devices in a mesh: fsdp: 32 (over y, z), tp: 8 (over x, core).
Axes of the slice: x: 4, y: 4, z: 8, core: 2. Of those that a mesh axis runs over, the one named last changes fastest.
Arguments:
- gradient: bfloat16 [256, 1024, 1024], P('tp', 'fsdp'), may hold values from -700 to 700
- slot_ids: int32 [256], P('tp'), may hold values from 0 to 63, as said below
- left_root: bfloat16 [512, 1024, 1024], P(('fsdp', 'tp')), may hold values from -0.1 to 4, as said below
- right_root: bfloat16 [512, 1024, 1024], P(('fsdp', 'tp')), may hold values from -0.1 to 4, as said below
Outputs:
- update: bfloat16 [256, 1024, 1024], P('tp', 'fsdp')
Inputs may be any that keep to these rules, and one draw needn't show every extreme that they name: `slot_ids`: blocks 32 * t to 32 * t + 31 form group t; within a group no two blocks share a value; value v names slot v % 2 of fsdp index v // 2; in every group some fsdp index receives 2 blocks. `left_root`: Symmetric, with the largest entries on the diagonal. `right_root`: Symmetric, with the largest entries on the diagonal.
All inputs are finite; a program needn't handle non-finite values.
Results may differ from a plain program's by a relative error of at most 0.0057.
Values may be sent and summed in bfloat16 or wider, within the bound.
A program may use at most 192 MiB of HBM per device.

v0:
```python
import jax
import jax.numpy as jnp
from jax import lax
from jax.sharding import PartitionSpec as P


def local(gradient, slot_ids, left_root, right_root):
    fsdp_size = lax.axis_size("fsdp")
    tp_size = lax.axis_size("tp")
    slot_count = left_root.shape[0]
    group = gradient.shape[0]
    rows = gradient.shape[1]
    width = gradient.shape[2]
    slot_range = jnp.arange(slot_count, dtype=jnp.int32)
    owner_range = jnp.arange(fsdp_size, dtype=jnp.int32)
    targets = (slot_range[:, None] + slot_count * owner_range[None, :]).reshape(-1)
    select = (slot_ids[None, :] == targets[:, None]).astype(jnp.bfloat16)
    outgoing = jnp.einsum(
        "qb,brc->qrc", select, gradient, preferred_element_type=jnp.float32
    ).astype(jnp.bfloat16)
    outgoing = outgoing.reshape(slot_count, fsdp_size * rows, width)
    owned = lax.all_to_all(outgoing, "fsdp", split_axis=1, concat_axis=1, tiled=True)
    inner = jnp.einsum("sij,sjk->sik", left_root, owned, preferred_element_type=jnp.float32).astype(
        jnp.bfloat16
    )
    direction = jnp.einsum(
        "sij,sjk->sik", inner, right_root, preferred_element_type=jnp.float32
    ).astype(jnp.bfloat16)
    returned = lax.all_to_all(direction, "fsdp", split_axis=1, concat_axis=1, tiled=True)
    returned = returned.reshape(slot_count * fsdp_size, rows, width)
    back = jnp.einsum("qb,qrc->brc", select, returned, preferred_element_type=jnp.float32).astype(
        jnp.bfloat16
    )
    wide_back = back.astype(jnp.float32)
    total = lax.psum(jnp.sum(wide_back * wide_back), ("fsdp", "tp"))
    count = group * tp_size * width * width
    factor = 0.5 / jnp.sqrt(total / count + 1e-06)
    return (wide_back * factor).astype(jnp.bfloat16)


def solution(mesh):
    placed = (
        P("tp", "fsdp", None),
        P("tp"),
        P(("fsdp", "tp"), None, None),
        P(("fsdp", "tp"), None, None),
    )
    return jax.shard_map(
        local, mesh=mesh, in_specs=placed, out_specs=P("tp", "fsdp", None), check_vma=False
    )
```

profile of v0, /device:TPU:1, one launch (start us, length us, event | category | flops | bytes accessed | tf_op | source)
XLA Modules:
  0.0 333.9 jit_solution(7233810825066969061)
XLA Ops:
  0.0 0.0 copy-start
  0.0 0.1 add.28
  0.1 1.5 copy-done
  1.6 3.9 %convolution_convert_fusion = bf16[64,32,1024]{2,0,1:T(8,128)(2,1)S(1)} fusion(bf16[32,32,1024]{2,1,0:T(8,128)(2,1)S(1)} %copy-done, s32[64]{0:T(128)S(1)} %add.28, s32[32]{0:T(128)} %param.5), kind=kOutput, calls=%fused_computation.11 | convolution fusion | flops 136316928 | bytes 6291840 | tf_op jit(solution)/shard_map/qb,brc->qrc/dot_general | solution.py:18
  5.5 2.3 copy.20
  7.8 6.3 %copy.21 = bf16[2,1024,1024]{2,0,1:T(2,128)(2,1)} copy(bf16[2,1024,1024]{2,1,0:T(8,128)(2,1)S(1)} %bitcast.11) | data formatting | bytes 8388608 | tf_op jit(solution)/shard_map/reshape | solution.py:21
  14.1 104.2 %all_to_all.10 = bf16[2,1024,1024]{2,0,1:T(2,128)(2,1)} all-to-all(bf16[2,1024,1024]{2,0,1:T(2,128)(2,1)} %copy.21), channel_id=1, replica_groups=mesh['fsdp'=32,'tp'=8] {'fsdp'}, dimensions={1} | all-to-all | bytes 8388608 | tf_op jit(solution)/shard_map/all_to_all | solution.py:22
  118.3 16.5 %fusion.8 = bf16[2,1024,1024]{2,1,0:T(8,128)(2,1)} fusion(bf16[2,1024,1024]{2,1,0:T(8,128)(2,1)} %param.7, bf16[2,1024,1024]{2,1,0:T(8,128)(2,1)} %param.6, bf16[2,1024,1024]{2,0,1:T(2,128)(2,1)} %all_to_all.10), kind=kOutput, calls=%fused_computation.10 | convolution fusion | flops 8594128896 | bytes 16777216 | tf_op jit(solution)/shard_map/sij,sjk->sik/dot_general | solution.py:26
  134.8 6.5 %copy.24 = bf16[2,1024,1024]{2,0,1:T(2,128)(2,1)S(1)} copy(bf16[2,1024,1024]{2,1,0:T(8,128)(2,1)} %fusion.8) | data formatting | bytes 8388608 | tf_op jit(solution)/shard_map/convert_element_type | solution.py:28
  141.3 100.6 %all_to_all.11 = bf16[2,1024,1024]{2,0,1:T(2,128)(2,1)S(1)} all-to-all(bf16[2,1024,1024]{2,0,1:T(2,128)(2,1)S(1)} %copy.24), channel_id=1, replica_groups=mesh['fsdp'=32,'tp'=8] {'fsdp'}, dimensions={1} | all-to-all | bytes 8388608 | tf_op jit(solution)/shard_map/all_to_all | solution.py:29
  241.9 0.0 copy-start.1
  241.9 1.3 copy.25
  243.2 0.0 copy-done.1
  243.2 7.1 %fusion = (f32[]{:T(128)}, bf16[32,32,1024]{2,0,1:T(8,128)(2,1)}) fusion(bf16[64,32,1024]{2,1,0:T(8,128)(2,1)S(1)} %bitcast.12, s32[64]{0:T(128)S(1)} %add.28, s32[32]{0:T(128)S(1)} %copy-done.1), kind=kOutput, calls=%fused_computation.2 | convolution fusion | flops 138414080 | bytes 6291844 | tf_op jit(solution)/shard_map/qb,qrc->brc/dot_general | solution.py:31
  250.3 78.4 %psum.7 = f32[]{:T(128)} all-reduce(f32[]{:T(128)} %get-tuple-element.5), channel_id=1, replica_groups=mesh['fsdp'=32,'tp'=8] {'fsdp','tp'}, use_global_device_ids=true, to_apply=%region_1.0 | all-reduce | flops 1 | bytes 8 | tf_op jit(solution)/shard_map/psum | solution.py:35
  329.3 2.1 fusion.1
  331.4 2.5 copy.27
  (2 shorter events, 0.0 us)
Async XLA Ops:
  0.0 1.6 copy-start
  241.9 1.3 copy-start.1
where the time goes:
time: 334 us
  blocking collectives  283 us (85%)
  matrix products  27.5 us (8%)
  local copies, waits for them, and re-layouts  20.5 us (6%)
    all_to_all x1, blocking collectives, local(): lax.all_to_all(outgoing, 'fsdp', split_axis=1, concat_axis=1, tiled=True)  104 us
    all_to_all x1, blocking collectives, local(): lax.all_to_all(direction, 'fsdp', split_axis=1, concat_axis=1, tiled=True)  101 us
    psum x1, blocking collectives, local(): total = lax.psum(jnp.sum(wide_back * wide_back), ('fsdp', 'tp'))  78.4 us
    dot_general x1, matrix products, local(): jnp.einsum('sij,sjk->sik', inner, right_root, preferred_element_type=jnp....  16.5 us
    dot_general x1, matrix products, local(): jnp.einsum('qb,qrc->brc', select, returned, preferred_element_type=jnp.fl...  7.1 us

commit v1 on v0

--- a/solution.py
+++ b/solution.py
@@ -1,10 +1,455 @@
 import jax
 import jax.numpy as jnp
 from jax import lax
+from jax.experimental import pallas as pl
+from jax.experimental.pallas import tpu as pltpu
 from jax.sharding import PartitionSpec as P
 
-
-def local(gradient, slot_ids, left_root, right_root):
+MESH = pl.DeviceIdType.MESH
+NF = 32
+NZ = 8
+NY = 4
+NT = 8
+BLOCKS = 32
+ROWS = 32
+W = 1024
+CW = 128
+SECONDS = 16
+LIST = 16
+BAND = 256
+HALF = 16
+PAIRS = NT * NY
+EARLY, MIDDLE = 6, 12
+
+BF16 = jnp.bfloat16
+F32 = jnp.float32
+I32 = jnp.int32
+
+FIRST, IDS, SUM_F, SUM_T = 0, 1, 2, 3
+BACK_FIRST, SPREAD, CROSS, COLLECT, BACK_COLLECT, BACK_CROSS, BACK_SPREAD, N_SEMS = range(4, 20, 2)
+GRAD, LEFT, RIGHT, TAB_A, TAB_B, OUT, OWN, N_LOCAL = range(8)
+T_FIRST, T_SEL, T_HAS1, T_HAS2, T_RANK, T_PLACE, T_SECOND, T_BACK, T_CROSS, T_RETURN, N_TABS = range(11)
+
+
+def dot(a, b):
+    return jnp.dot(a, b, preferred_element_type=F32)
+
+
+def within(index, size):
+    return jnp.clip(index, 0, size - 1)
+
+
+def owners(ids):
+    lane = lax.broadcasted_iota(I32, (8, 128), 1)
+    zero = jnp.zeros((8, 128), F32)
+    p0, p1, b0, b1 = zero, zero, zero, zero
+    for b in range(BLOCKS):
+        column = jnp.broadcast_to(ids[:, b : b + 1], (8, 128))
+        e0 = jnp.where(column == 2 * lane, 1.0, 0.0)
+        e1 = jnp.where(column == 2 * lane + 1, 1.0, 0.0)
+        p0, p1 = jnp.maximum(p0, e0), jnp.maximum(p1, e1)
+        b0, b1 = b0 + b * e0, b1 + b * e1
+    has2 = p0 * p1
+    earlier = lax.broadcasted_iota(I32, (128, 128), 0) < lax.broadcasted_iota(I32, (128, 128), 1)
+    rank = dot(has2.astype(BF16), jnp.where(earlier, 1.0, 0.0).astype(BF16))
+    first = jnp.clip(p0 * b0 + (1.0 - p0) * b1, 0.0, BLOCKS - 1.0)
+    return p0, p1, first, b1, has2, rank
+
+
+def by_rank(has2, rank, value, highest):
+    lane = lax.broadcasted_iota(I32, (8, 128), 1)
+    table = jnp.zeros((8, 128), F32)
+    for j in range(SECONDS):
+        found = jnp.sum(jnp.where(rank == float(j), has2 * value, 0.0), axis=1, keepdims=True)
+        table = jnp.where(lane == j, jnp.broadcast_to(found, (8, 128)), table)
+    return jnp.clip(table, 0.0, float(highest)).astype(I32)
+
+
+def by_place(has2, place, value, highest):
+    row = lax.broadcasted_iota(I32, (16, 128), 0)
+    rows = jnp.zeros((16, 128), F32)
+    for i in range(LIST):
+        found = jnp.sum(jnp.where(place == float(i), has2 * value, 0.0), axis=0, keepdims=True)
+        rows = jnp.where(row == i, jnp.broadcast_to(found, (16, 128)), rows)
+    source = lax.broadcasted_iota(I32, (128, 128), 0)
+    target = lax.broadcasted_iota(I32, (128, 128), 1)
+    fold = jnp.where((source % NZ == target) & (source < NF), 1.0, 0.0).astype(BF16)
+    return jnp.clip(dot(rows.astype(BF16), fold), 0.0, float(highest)).astype(I32)
+
+
+def kernel(
+    ids_ref, ids_smem, grad_hbm, left_hbm, right_hbm, out_hbm, flag_ref,
+    grad, left, right, snd0, rcv0, sp_snd, sp_rcv, z_snd, z_rcv, c_snd, rcv1, inner, dir0, dir1,
+    ret0, rc, rz_snd, rz_rcv, rs_snd, rs_rcv, outv, ids_snd, ids_all, tab_a, tab_b, tab_as, tab_bs,
+    part_f, part_t, sum_f, sum_t, ss, rs, ls,
+):
+    f = lax.axis_index("fsdp")
+    t = lax.axis_index("tp")
+    y, z = f // NZ, f % NZ
+
+    def shifted(k):
+        return lax.rem(y + k // NZ, NY) * NZ + lax.rem(z + lax.rem(k, NZ), NZ)
+
+    def tp_shifted(k):
+        return lax.rem(t + k, NT)
+
+    def z_shifted(k):
+        return lax.rem(z + k, NZ)
+
+    def send(source, target, phase, to_f, to_t):
+        pltpu.make_async_remote_copy(
+            src_ref=source, dst_ref=target, send_sem=ss.at[phase], recv_sem=rs.at[phase],
+            device_id=(to_f, to_t), device_id_type=MESH,
+        ).start()
+
+    def own(source, target, phase):
+        pltpu.make_async_copy(source, target, rs.at[phase]).start()
+
+    def wait(ref, sem):
+        pltpu.make_async_copy(ref, ref, sem).wait()
+
+    def loop(lowest, highest, body):
+        def step(k, carry):
+            body(k)
+            return carry
+
+        lax.fori_loop(lowest, highest, step, 0)
+
+    load_grad = pltpu.make_async_copy(grad_hbm, grad, ls.at[GRAD])
+    load_left = pltpu.make_async_copy(left_hbm, left, ls.at[LEFT])
+    load_right = pltpu.make_async_copy(right_hbm, right, ls.at[RIGHT])
+    load_grad.start()
+
+    barrier = pltpu.get_barrier_semaphore()
+
+    def greet_f(k):
+        pl.semaphore_signal(barrier, inc=1, device_id=(shifted(k), t), device_id_type=MESH)
+
+    def greet_t(k):
+        pl.semaphore_signal(
+            barrier, inc=1, device_id=(lax.rem(y + lax.rem(k, NY), NY) * NZ + z, tp_shifted(k // NY)), device_id_type=MESH
+        )
+
+    loop(1, NF, greet_f)
+    loop(NY, PAIRS, greet_t)
+    load_left.start()
+    load_right.start()
+
+    ids_snd[...] = jnp.full((8, 128), -1, I32)
+    ids_snd[:, :BLOCKS] = jnp.broadcast_to(ids_ref[...], (8, BLOCKS))
+    p0, p1, first, second, has2, rank = owners(ids_snd[...])
+    tab_a[0] = first.astype(I32)
+    tab_a[1] = by_rank(has2, rank, second, BLOCKS - 1)
+    copy_a = pltpu.make_async_copy(tab_a, tab_as, ls.at[TAB_A])
+    copy_a.start()
+    ids_all[t] = ids_snd[...]
+    pl.semaphore_wait(barrier, NF - 1 + PAIRS - NY)
+
+    def send_ids(k):
+        send(ids_snd, ids_all.at[t], IDS, f, tp_shifted(k))
+
+    loop(1, NT, send_ids)
+    copy_a.wait()
+    load_grad.wait()
+
+    def pack_spread(j):
+        b = within(tab_as[1, 0, j], BLOCKS)
+        for h in range(2):
+            for r in range(NT):
+                sp_snd[h][r * SECONDS + j] = grad[b, h * HALF : (h + 1) * HALF, r * CW : (r + 1) * CW]
+
+    def spread(source, target, phase, h):
+        def one(k):
+            to = tp_shifted(k)
+            send(source[h].at[pl.ds(to * SECONDS, SECONDS)], target[h].at[pl.ds(t * SECONDS, SECONDS)], phase + h, f, to)
+
+        loop(1, NT, one)
+        mine = pl.ds(t * SECONDS, SECONDS)
+        own(source[h].at[mine], target[h].at[mine], phase + h)
+
+    def cross(source, target, phase, h):
+        def one(k):
+            to = z_shifted(k)
+            send(source[h].at[pl.ds(to * LIST, LIST)], target[h].at[pl.ds(z * LIST, LIST)], phase + h, y * NZ + to, t)
+
+        loop(1, NZ, one)
+        mine = pl.ds(z * LIST, LIST)
+        own(source[h].at[mine], target[h].at[mine], phase + h)
+
+    loop(0, SECONDS, pack_spread)
+    spread(sp_snd, sp_rcv, SPREAD, 0)
+    spread(sp_snd, sp_rcv, SPREAD, 1)
+
+    def send_first(k):
+        to = shifted(k)
+        snd0[to] = grad[within(tab_as[0, 0, to], BLOCKS)]
+        send(snd0.at[to], rcv0.at[pl.ds(f * ROWS, ROWS)], FIRST, to, t)
+
+    loop(1, EARLY, send_first)
+
+    wait(ids_all.at[pl.ds(0, NT - 1)], rs.at[IDS])
+    row = lax.broadcasted_iota(I32, (8, 128), 0)
+    ids = jnp.zeros((8, 128), I32)
+    for g in range(NT):
+        ids = jnp.where(row == g, ids_all[g], ids)
+    p0, p1, first, second, has2, rank = owners(ids)
+    source = lax.broadcasted_iota(I32, (128, 128), 0)
+    target = lax.broadcasted_iota(I32, (128, 128), 1)
+    plane = jnp.where((source % NZ == target % NZ) & (source < NF), 1.0, 0.0)
+    before = jnp.where(source // NZ < target // NZ, plane, 0.0)
+    in_plane = dot(has2.astype(BF16), plane.astype(BF16))
+    place = dot(has2.astype(BF16), before.astype(BF16))
+    for g in range(NT - 1):
+        place = place + jnp.where(row > g, jnp.broadcast_to(in_plane[g : g + 1, :], (8, 128)), 0.0)
+    longest = jnp.max(jnp.sum(in_plane, axis=0, keepdims=True), axis=1, keepdims=True)
+    flag_ref[0, 0] = jnp.max(longest.astype(I32))
+    bounded = jnp.clip(place, 0.0, LIST - 1.0)
+    group = row.astype(F32)
+    lane = lax.broadcasted_iota(I32, (8, 128), 1)
+    tab_b[...] = jnp.zeros_like(tab_b)
+    tab_b[T_SEL, :8] = (1.0 - p0).astype(I32)
+    tab_b[T_HAS1, :8] = jnp.maximum(p0, p1).astype(I32)
+    tab_b[T_HAS2, :8] = has2.astype(I32)
+    tab_b[T_RANK, :8] = jnp.clip(rank, 0.0, SECONDS - 1.0).astype(I32)
+    tab_b[T_PLACE, :8] = bounded.astype(I32)
+    tab_b[T_BACK, :8] = by_rank(has2, rank, (lane % NZ).astype(F32) * LIST + bounded, NZ * LIST - 1)
+    tab_b[T_CROSS] = by_place(has2, place, group * SECONDS + rank, NT * SECONDS - 1)
+    tab_b[T_RETURN] = by_place(has2, place, group * NY + (lane // NZ).astype(F32), PAIRS - 1)
+    copy_b = pltpu.make_async_copy(tab_b, tab_bs, ls.at[TAB_B])
+    copy_b.start()
+    copy_b.wait()
+
+    def pack_cross(h):
+        def one(k):
+            z_snd[h][k] = sp_rcv[h][within(tab_bs[T_CROSS, k % LIST, k // LIST], NT * SECONDS)]
+
+        loop(0, NZ * LIST, one)
+
+    for h, lowest, highest in ((0, EARLY, MIDDLE), (1, MIDDLE, NF)):
+        wait(sp_rcv[h], rs.at[SPREAD + h])
+        pack_cross(h)
+        cross(z_snd, z_rcv, CROSS, h)
+        loop(lowest, highest, send_first)
+    snd0[f] = grad[within(tab_as[0, 0, f], BLOCKS)]
+    own(snd0.at[f], rcv0.at[pl.ds(f * ROWS, ROWS)], FIRST)
+
+    here = t * NY + y
+
+    def pack_collect(h):
+        def one(q):
+            place_q = within(tab_bs[T_PLACE, q // NY, (q % NY) * NZ + z], LIST)
+            for s in range(NZ):
+                c_snd[h][q, s] = z_rcv[h][s * LIST + place_q]
+
+        loop(0, PAIRS, one)
+
+    def collect(h):
+        def one(k):
+            to_t, to_y = tp_shifted(k // NY), lax.rem(y + lax.rem(k, NY), NY)
+            send(c_snd[h].at[to_t * NY + to_y], rcv1.at[t, pl.ds(y * NZ, NZ), h], COLLECT + h, to_y * NZ + z, to_t)
+
+        loop(1, PAIRS, one)
+        own(c_snd[h].at[here], rcv1.at[t, pl.ds(y * NZ, NZ), h], COLLECT + h)
+
+    for h in range(2):
+        wait(z_rcv[h], rs.at[CROSS + h])
+        pack_collect(h)
+        collect(h)
+
+    load_left.wait()
+    load_right.wait()
+    wait(rcv1.at[:, :, 0], rs.at[COLLECT])
+    wait(rcv1.at[:, :, 1], rs.at[COLLECT + 1])
+
+    def squares(total, part):
+        wide = part.astype(F32)
+        return total + jnp.sum((wide * wide).reshape(BAND // 8, 8, BAND), axis=0)
+
+    def back_collect(to_y, to_t, h):
+        send(dir1.at[to_t, pl.ds(to_y * NZ, NZ), h], rc[h].at[here], BACK_COLLECT + h, to_y * NZ + z, to_t)
+
+    def second_band(k, total):
+        to_y = lax.rem(y + k, NY)
+        rows = pl.ds(to_y * BAND, BAND)
+        lhs = left[1, rows, :]
+        for c in range(W // BAND):
+            rhs = jnp.concatenate([rcv1[2 * c].reshape(W, CW), rcv1[2 * c + 1].reshape(W, CW)], axis=1)
+            inner[:, c * BAND : (c + 1) * BAND] = dot(lhs, rhs).astype(BF16)
+        mid = inner[...]
+        for c in range(W // BAND):
+            part = dot(mid, right[1, :, c * BAND : (c + 1) * BAND]).astype(BF16)
+            for i in range(2):
+                dir1[2 * c + i, pl.ds(to_y * NZ, NZ)] = part[:, i * CW : (i + 1) * CW].reshape(NZ, 2, HALF, CW)
+            total = squares(total, part)
+        loop(jnp.where(k == 0, 1, 0), NT, lambda r: back_collect(to_y, tp_shifted(r), 0))
+        return total
+
+    zeros = jnp.zeros((8, BAND), F32)
+    sum1 = lax.fori_loop(0, NY, second_band, zeros)
+    loop(1, PAIRS, lambda k: back_collect(lax.rem(y + lax.rem(k, NY), NY), tp_shifted(k // NY), 1))
+    for h in range(2):
+        own(dir1.at[t, pl.ds(y * NZ, NZ), h], rc[h].at[here], BACK_COLLECT + h)
+
+    wait(rcv0, rs.at[FIRST])
+    which = within(tab_bs[T_SEL, t, f], 2)
+
+    def back_first(k, h):
+        to = shifted(k)
+        send(dir0.at[pl.ds(to * ROWS + h * HALF, HALF)], ret0[h].at[f], BACK_FIRST + h, to, t)
+
+    def first_band(k, total):
+        rows = pl.ds(lax.rem(y + k, NY) * BAND, BAND)
+        lhs = left[which, rows, :]
+        for c in range(W // BAND):
+            inner[:, c * BAND : (c + 1) * BAND] = dot(lhs, rcv0[:, c * BAND : (c + 1) * BAND]).astype(BF16)
+        mid = inner[...]
+        for c in range(W // BAND):
+            part = dot(mid, right[which, :, c * BAND : (c + 1) * BAND]).astype(BF16)
+            dir0[rows, c * BAND : (c + 1) * BAND] = part
+            total = squares(total, part)
+        loop(jnp.where(k == 0, 1, 0), NZ, lambda s: back_first(k * NZ + s, 0))
+        return total
+
+    sum0 = lax.fori_loop(0, NY, first_band, zeros)
+    for h in range(2):
+        own(dir0.at[pl.ds(f * ROWS + h * HALF, HALF)], ret0[h].at[f], BACK_FIRST + h)
+
+    kept = jnp.where(tab_bs[T_HAS1, t, f] > 0, sum0, 0.0) + jnp.where(tab_bs[T_HAS2, t, f] > 0, sum1, 0.0)
+    part_f[...] = kept[:, :128] + kept[:, 128:]
+    sum_f[f] = part_f[...]
+    loop(1, NF, lambda k: send(part_f, sum_f.at[f], SUM_F, shifted(k), t))
+
+    def pack_back_cross(h):
+        def one(k):
+            rz_snd[h][k] = rc[h][within(tab_bs[T_RETURN, k % LIST, z], PAIRS), k // LIST]
+
+        loop(0, NZ * LIST, one)
+
+    for h in range(2):
+        wait(rc[h], rs.at[BACK_COLLECT + h])
+        pack_back_cross(h)
+        cross(rz_snd, rz_rcv, BACK_CROSS, h)
+
+    loop(1, NF, lambda k: back_first(k, 1))
+
+    wait(sum_f.at[pl.ds(0, NF - 1)], rs.at[SUM_F])
+    part_t[...] = jnp.sum(sum_f[...], axis=0)
+    sum_t[t] = part_t[...]
+    loop(1, NT, lambda k: send(part_t, sum_t.at[t], SUM_T, f, tp_shifted(k)))
+
+    def pack_back_spread(h):
+        def one(k):
+            rs_snd[h][k] = rz_rcv[h][within(tab_bs[T_BACK, k // SECONDS, k % SECONDS], NZ * LIST)]
+
+        loop(0, NT * SECONDS, one)
+
+    for h in range(2):
+        wait(rz_rcv[h], rs.at[BACK_CROSS + h])
+        pack_back_spread(h)
+        spread(rs_snd, rs_rcv, BACK_SPREAD, h)
+
+    wait(sum_t.at[pl.ds(0, NT - 1)], rs.at[SUM_T])
+    total = jnp.full((8, 128), jnp.sum(jnp.sum(sum_t[...], axis=0)))
+    factor = 0.5 / jnp.sqrt(total / float(NT * BLOCKS * W * W) + 1e-6)
+    scale = jnp.broadcast_to(factor[:1, :], (HALF, CW))
+
+    def finish(h):
+        def one(b):
+            v = within(ids_smem[b], 2 * NF)
+            o = v // 2
+            is_second = (v % 2) * tab_bs[T_HAS2, t, o]
+            j = within(is_second * tab_bs[T_RANK, t, o], SECONDS)
+            rows = slice(h * HALF, (h + 1) * HALF)
+            for r in range(NT):
+                columns = slice(r * CW, (r + 1) * CW)
+                value = jnp.where(is_second > 0, rs_rcv[h][r * SECONDS + j], ret0[h][o, :, columns])
+                outv[b, rows, columns] = (value.astype(F32) * scale).astype(BF16)
+            pltpu.make_async_copy(outv.at[b, rows], out_hbm.at[b, rows], ls.at[OUT]).start()
+
+        loop(0, BLOCKS, one)
+
+    for h in range(2):
+        wait(rs_rcv[h], rs.at[BACK_SPREAD + h])
+        wait(ret0[h], rs.at[BACK_FIRST + h])
+        finish(h)
+    wait(outv, ls.at[OUT])
+
+    wait(snd0.at[pl.ds(0, NF - 1)], ss.at[FIRST])
+    for h in range(2):
+        wait(ret0[h].at[pl.ds(0, NF - 1)], ss.at[BACK_FIRST + h])
+        for phase in (SPREAD, CROSS, BACK_CROSS, BACK_SPREAD):
+            wait(sp_snd[h].at[pl.ds(0, (NT - 1) * SECONDS)], ss.at[phase + h])
+        for phase in (COLLECT, BACK_COLLECT):
+            wait(c_snd[h].at[pl.ds(0, PAIRS - 1)], ss.at[phase + h])
+    wait(ids_all.at[pl.ds(0, NT - 1)], ss.at[IDS])
+    wait(sum_f.at[pl.ds(0, NF - 1)], ss.at[SUM_F])
+    wait(sum_t.at[pl.ds(0, NT - 1)], ss.at[SUM_T])
+
+
+def packed(gradient, slot_ids, left_root, right_root):
+    piece = (pltpu.VMEM((NT * SECONDS, HALF, CW), BF16),) * 2
+    matrix = pltpu.VMEM((W, W), BF16)
+    rows = pltpu.VMEM((NF, ROWS, W), BF16)
+    columns = pltpu.VMEM((NT, NF, 2, HALF, CW), BF16)
+    plane = (pltpu.VMEM((PAIRS, NZ, HALF, CW), BF16),) * 2
+    roots = pltpu.VMEM((2, W, W), BF16)
+    return pl.pallas_call(
+        kernel,
+        out_shape=(
+            jax.ShapeDtypeStruct((BLOCKS, ROWS, W), BF16),
+            jax.ShapeDtypeStruct((1, 1), I32),
+        ),
+        in_specs=[
+            pl.BlockSpec(memory_space=pltpu.VMEM),
+            pl.BlockSpec(memory_space=pltpu.SMEM),
+            pl.BlockSpec(memory_space=pl.ANY),
+            pl.BlockSpec(memory_space=pl.ANY),
+            pl.BlockSpec(memory_space=pl.ANY),
+        ],
+        out_specs=(pl.BlockSpec(memory_space=pl.ANY), pl.BlockSpec(memory_space=pltpu.SMEM)),
+        scratch_shapes=[
+            rows,
+            roots,
+            roots,
+            rows,
+            matrix,
+            piece,
+            piece,
+            piece,
+            piece,
+            plane,
+            columns,
+            pltpu.VMEM((BAND, W), BF16),
+            matrix,
+            columns,
+            (pltpu.VMEM((NF, HALF, W), BF16),) * 2,
+            plane,
+            piece,
+            piece,
+            piece,
+            piece,
+            rows,
+            pltpu.VMEM((8, 128), I32),
+            pltpu.VMEM((NT, 8, 128), I32),
+            pltpu.VMEM((2, 8, 128), I32),
+            pltpu.VMEM((N_TABS, 16, 128), I32),
+            pltpu.SMEM((2, 8, 128), I32),
+            pltpu.SMEM((N_TABS, 16, 128), I32),
+            pltpu.VMEM((8, 128), F32),
+            pltpu.VMEM((8, 128), F32),
+            pltpu.VMEM((NF, 8, 128), F32),
+            pltpu.VMEM((NT, 8, 128), F32),
+            pltpu.SemaphoreType.DMA((N_SEMS,)),
+            pltpu.SemaphoreType.DMA((N_SEMS,)),
+            pltpu.SemaphoreType.DMA((N_LOCAL,)),
+        ],
+        compiler_params=pltpu.CompilerParams(
+            collective_id=0, has_side_effects=True, vmem_limit_bytes=56 * 2**20
+        ),
+    )(slot_ids.reshape(1, BLOCKS), slot_ids, gradient, left_root, right_root)
+
+
+def plain(gradient, slot_ids, left_root, right_root):
     fsdp_size = lax.axis_size("fsdp")
     tp_size = lax.axis_size("tp")
     slot_count = left_root.shape[0]
@@ -38,6 +483,16 @@
     return (wide_back * factor).astype(jnp.bfloat16)
 
 
+def local(gradient, slot_ids, left_root, right_root):
+    update, longest = packed(gradient, slot_ids, left_root, right_root)
+    return lax.cond(
+        longest[0, 0] > LIST,
+        lambda u, *args: plain(*args),
+        lambda u, *args: u,
+        update, gradient, slot_ids, left_root, right_root,
+    )
+
+
 def solution(mesh):
     placed = (
         P("tp", "fsdp", None),

time: 334 us -> 181 us (0.54)
  the two profiles are of different devices: /device:TPU:1 before, /device:TPU:202 now
where the time goes in v1:
time: 181 us
  Pallas kernels  179 us (99%)
    pallas_call x1, Pallas kernels, packed(): pl.pallas_call(kernel, out_shape=(jax.ShapeDtypeStruct((BLOCKS, ROWS, W),...  179 us

profile of v1, /device:TPU:202, one launch (start us, length us, event | category | flops | bytes accessed | tf_op | source)
XLA Modules:
  0.0 181.2 jit_solution(13045262386412667547)
XLA Ops:
  0.0 0.0 copy-start
  0.0 0.0 copy-start.1
  0.0 179.1 %shard_map.48 = (bf16[32,32,1024]{2,1,0:T(8,128)(2,1)S(1)}, s32[1,1]{1,0:T(1,128)}) custom-call(s32[1,32]{1,0:T(1,128)} %bitcast.15, s32[32]{0:T(128)} %ids_smem.1, bf16[32,32,1024]{2,1,0:T(8,128)(2,1)} %grad_hbm.1, bf16[2,1024,1024]{2,1,0:T(8,128)(2,1)} %left_hbm.1, bf16[2,1024,1024]{2,1,0:T(8,128)(2,1)} %right_hbm.1), custom_call_target="tpu_custom_call" | custom-call | tf_op jit(solution)/shard_map/pallas_call | solution.py:396
  179.6 0.0 copy-done
  179.6 0.0 copy-done.1
  179.6 0.2 conditional.1
  179.9 1.3 copy.54
Async XLA Ops:
  0.0 179.6 %copy-start = (bf16[32,32,1024]{2,1,0:T(8,128)(2,1)S(1)}, bf16[32,32,1024]{2,1,0:T(8,128)(2,1)}, u32[]{:S(2)}) copy-start(bf16[32,32,1024]{2,1,0:T(8,128)(2,1)} %grad_hbm.1) | copy-start | bytes 6291460
  0.0 179.6 %copy-start.1 = (s32[32]{0:T(128)S(1)}, s32[32]{0:T(128)}, u32[]{:S(2)}) copy-start(s32[32]{0:T(128)} %ids_smem.1) | copy-start | bytes 388

commit v2 on v1

--- a/solution.py
+++ b/solution.py
@@ -19,7 +19,7 @@
 BAND = 256
 HALF = 16
 PAIRS = NT * NY
-EARLY, MIDDLE = 6, 12
+PORTIONS = (1, 6, 12, 18, 24, NF)
 
 BF16 = jnp.bfloat16
 F32 = jnp.float32
@@ -143,12 +143,10 @@
     copy_a = pltpu.make_async_copy(tab_a, tab_as, ls.at[TAB_A])
     copy_a.start()
     ids_all[t] = ids_snd[...]
-    pl.semaphore_wait(barrier, NF - 1 + PAIRS - NY)
 
     def send_ids(k):
         send(ids_snd, ids_all.at[t], IDS, f, tp_shifted(k))
 
-    loop(1, NT, send_ids)
     copy_a.wait()
     load_grad.wait()
 
@@ -176,16 +174,23 @@
         mine = pl.ds(z * LIST, LIST)
         own(source[h].at[mine], target[h].at[mine], phase + h)
 
+    def pack_first(o):
+        snd0[o] = grad[within(tab_as[0, 0, o], BLOCKS)]
+
+    def send_first(k):
+        to = shifted(k)
+        send(snd0.at[to], rcv0.at[pl.ds(f * ROWS, ROWS)], FIRST, to, t)
+
+    def send_portion(i):
+        loop(PORTIONS[i], PORTIONS[i + 1], send_first)
+
     loop(0, SECONDS, pack_spread)
+    loop(0, NF, pack_first)
+    pl.semaphore_wait(barrier, NF - 1 + PAIRS - NY)
+    loop(1, NT, send_ids)
     spread(sp_snd, sp_rcv, SPREAD, 0)
     spread(sp_snd, sp_rcv, SPREAD, 1)
-
-    def send_first(k):
-        to = shifted(k)
-        snd0[to] = grad[within(tab_as[0, 0, to], BLOCKS)]
-        send(snd0.at[to], rcv0.at[pl.ds(f * ROWS, ROWS)], FIRST, to, t)
-
-    loop(1, EARLY, send_first)
+    send_portion(0)
 
     wait(ids_all.at[pl.ds(0, NT - 1)], rs.at[IDS])
     row = lax.broadcasted_iota(I32, (8, 128), 0)
@@ -225,12 +230,11 @@
 
         loop(0, NZ * LIST, one)
 
-    for h, lowest, highest in ((0, EARLY, MIDDLE), (1, MIDDLE, NF)):
+    for h in range(2):
         wait(sp_rcv[h], rs.at[SPREAD + h])
         pack_cross(h)
         cross(z_snd, z_rcv, CROSS, h)
-        loop(lowest, highest, send_first)
-    snd0[f] = grad[within(tab_as[0, 0, f], BLOCKS)]
+        send_portion(1 + h)
     own(snd0.at[f], rcv0.at[pl.ds(f * ROWS, ROWS)], FIRST)
 
     here = t * NY + y
@@ -255,6 +259,7 @@
         wait(z_rcv[h], rs.at[CROSS + h])
         pack_collect(h)
         collect(h)
+        send_portion(3 + h)
 
     load_left.wait()
     load_right.wait()

time: 181 us -> 180 us (level)
  the two profiles are of different devices: /device:TPU:202 before, /device:TPU:1 now
where the time goes in v2:
time: 180 us; the launch traced here: 177 us
  Pallas kernels  175 us (97%)
    pallas_call x1, Pallas kernels, packed(): pl.pallas_call(kernel, out_shape=(jax.ShapeDtypeStruct((BLOCKS, ROWS, W),...  175 us

profile of v2, /device:TPU:1, one launch (start us, length us, event | category | flops | bytes accessed | tf_op | source)
XLA Modules:
  0.0 177.0 jit_solution(16531916136565917844)
XLA Ops:
  0.0 0.0 copy-start
  0.0 0.0 copy-start.1
  0.0 174.8 %shard_map.48 = (bf16[32,32,1024]{2,1,0:T(8,128)(2,1)S(1)}, s32[1,1]{1,0:T(1,128)}) custom-call(s32[1,32]{1,0:T(1,128)} %bitcast.15, s32[32]{0:T(128)} %ids_smem.1, bf16[32,32,1024]{2,1,0:T(8,128)(2,1)} %grad_hbm.1, bf16[2,1024,1024]{2,1,0:T(8,128)(2,1)} %left_hbm.1, bf16[2,1024,1024]{2,1,0:T(8,128)(2,1)} %right_hbm.1), custom_call_target="tpu_custom_call" | custom-call | tf_op jit(solution)/shard_map/pallas_call | solution.py:401
  175.4 0.0 copy-done
  175.4 0.0 copy-done.1
  175.4 0.2 conditional.1
  175.7 1.3 copy.54
Async XLA Ops:
  0.0 175.4 %copy-start = (bf16[32,32,1024]{2,1,0:T(8,128)(2,1)S(1)}, bf16[32,32,1024]{2,1,0:T(8,128)(2,1)}, u32[]{:S(2)}) copy-start(bf16[32,32,1024]{2,1,0:T(8,128)(2,1)} %grad_hbm.1) | copy-start | bytes 6291460
  0.0 175.4 %copy-start.1 = (s32[32]{0:T(128)S(1)}, s32[32]{0:T(128)}, u32[]{:S(2)}) copy-start(s32[32]{0:T(128)} %ids_smem.1) | copy-start | bytes 388

commit v3 on v2

--- a/solution.py
+++ b/solution.py
@@ -87,14 +87,22 @@
     t = lax.axis_index("tp")
     y, z = f // NZ, f % NZ
 
+    def both_ways(k, n):
+        odd = lax.rem(k, 2)
+        return odd * ((k + 1) // 2) + (1 - odd) * (n - k // 2)
+
+    def tp_shifted(k):
+        return lax.rem(t + both_ways(k, NT), NT)
+
+    def z_shifted(k):
+        return lax.rem(z + both_ways(k, NZ), NZ)
+
     def shifted(k):
-        return lax.rem(y + k // NZ, NY) * NZ + lax.rem(z + lax.rem(k, NZ), NZ)
-
-    def tp_shifted(k):
-        return lax.rem(t + k, NT)
-
-    def z_shifted(k):
-        return lax.rem(z + k, NZ)
+        return lax.rem(y + k // NZ, NY) * NZ + z_shifted(lax.rem(k, NZ))
+
+    def pair(k):
+        near = lax.rem(k, NT)
+        return tp_shifted(near), lax.rem(y + lax.rem(k // NT + near, NY), NY)
 
     def send(source, target, phase, to_f, to_t):
         pltpu.make_async_remote_copy(
@@ -249,7 +257,7 @@
 
     def collect(h):
         def one(k):
-            to_t, to_y = tp_shifted(k // NY), lax.rem(y + lax.rem(k, NY), NY)
+            to_t, to_y = pair(k)
             send(c_snd[h].at[to_t * NY + to_y], rcv1.at[t, pl.ds(y * NZ, NZ), h], COLLECT + h, to_y * NZ + z, to_t)
 
         loop(1, PAIRS, one)
@@ -291,7 +299,7 @@
 
     zeros = jnp.zeros((8, BAND), F32)
     sum1 = lax.fori_loop(0, NY, second_band, zeros)
-    loop(1, PAIRS, lambda k: back_collect(lax.rem(y + lax.rem(k, NY), NY), tp_shifted(k // NY), 1))
+    loop(1, PAIRS, lambda k: back_collect(pair(k)[1], pair(k)[0], 1))
     for h in range(2):
         own(dir1.at[t, pl.ds(y * NZ, NZ), h], rc[h].at[here], BACK_COLLECT + h)
 

time: 180 us -> 184 us (1.022)
  the two profiles are of different devices: /device:TPU:1 before, /device:TPU:68 now
where the time goes in v3:
time: 184 us
  Pallas kernels  182 us (99%)
    pallas_call x1, Pallas kernels, packed(): pl.pallas_call(kernel, out_shape=(jax.ShapeDtypeStruct((BLOCKS, ROWS, W),...  182 us

profile of v3, /device:TPU:68, one launch (start us, length us, event | category | flops | bytes accessed | tf_op | source)
XLA Modules:
  0.0 184.0 jit_solution(17306994178954833802)
XLA Ops:
  0.0 0.0 copy-start
  0.0 0.0 copy-start.1
  0.0 181.9 %shard_map.48 = (bf16[32,32,1024]{2,1,0:T(8,128)(2,1)S(1)}, s32[1,1]{1,0:T(1,128)}) custom-call(s32[1,32]{1,0:T(1,128)} %bitcast.15, s32[32]{0:T(128)} %ids_smem.1, bf16[32,32,1024]{2,1,0:T(8,128)(2,1)} %grad_hbm.1, bf16[2,1024,1024]{2,1,0:T(8,128)(2,1)} %left_hbm.1, bf16[2,1024,1024]{2,1,0:T(8,128)(2,1)} %right_hbm.1), custom_call_target="tpu_custom_call" | custom-call | tf_op jit(solution)/shard_map/pallas_call | solution.py:409
  182.4 0.0 copy-done
  182.4 0.0 copy-done.1
  182.5 0.2 conditional.1
  182.7 1.3 copy.54
Async XLA Ops:
  0.0 182.4 %copy-start = (bf16[32,32,1024]{2,1,0:T(8,128)(2,1)S(1)}, bf16[32,32,1024]{2,1,0:T(8,128)(2,1)}, u32[]{:S(2)}) copy-start(bf16[32,32,1024]{2,1,0:T(8,128)(2,1)} %grad_hbm.1) | copy-start | bytes 6291460
  0.0 182.4 %copy-start.1 = (s32[32]{0:T(128)S(1)}, s32[32]{0:T(128)}, u32[]{:S(2)}) copy-start(s32[32]{0:T(128)} %ids_smem.1) | copy-start | bytes 388
